TPU v7x, 512 devices: a whole 4x8x8 slice. The times are simulated.
512 devices in a mesh: patch: 64 (over z_lo, y, core), tp: 8 (over z_hi, x).
Axes of the slice: x: 4, y: 8, z: 8 (z_hi: 2, z_lo: 4; z = z_hi * 4 + z_lo), core: 2. Of those that a mesh axis runs over, the one named last changes fastest.
Arguments:
- queries: bfloat16 [2, 2048, 2048], P(None, 'patch', 'tp'), may hold values from -8 to 8
- new_keys: bfloat16 [2, 2048, 2048], P(None, 'patch', 'tp'), may hold values from -4 to 4
- new_values: bfloat16 [2, 2048, 2048], P(None, 'patch', 'tp'), may hold values from -6 to 6
- prev_keys: bfloat16 [2048, 2048], P('patch', 'tp'), may hold values from -4 to 4
- prev_values: bfloat16 [2048, 2048], P('patch', 'tp'), may hold values from -6 to 6
- kv_basis: bfloat16 [2, 16, 128, 32], P(None, 'tp'), may hold values from -0.5 to 0.5
- out_weight: bfloat16 [2048, 3072], P('tp'), may hold values from -0.1875 to 0.1875
- out_gate: float32 [2, 3072], P(None, 'tp'), may hold values from 0.5 to 1.5
Outputs:
- block_output: bfloat16 [2, 2048, 3072], P(None, 'patch', 'tp')
All inputs are finite; a program needn't handle non-finite values.
Results may differ from a plain program's by a relative error of at most 0.018.
The roundings to bfloat16 on the way count: a program that leaves them out, or rounds other values in their place, can miss the bound.
Values may be sent and summed in bfloat16 or wider, within the bound.
A program may use at most 64 MiB of HBM per device.

v0:
```python
import jax
import jax.numpy as jnp
from jax import lax
from jax.sharding import PartitionSpec as P


def take_rows(array, offset, row_count):
    return lax.dynamic_slice_in_dim(array, offset, row_count, 0)


def project(fresh_rows, shared, basis_one, head_count):
    residual = (fresh_rows.astype(jnp.float32) - shared.astype(jnp.float32)).reshape(
        fresh_rows.shape[0], head_count, -1
    )
    return jnp.einsum(
        "thd,hdr->thr", residual, basis_one.astype(jnp.float32), precision=lax.Precision.HIGHEST
    ).astype(jnp.bfloat16)


def basis_maps(kv_basis):
    head_count = kv_basis.shape[1]
    head_dim = kv_basis.shape[2]
    rank_count = kv_basis.shape[3]
    identity = jnp.eye(head_count, dtype=jnp.bfloat16)
    blocks = []
    for member in range(2):
        diagonal_block = jnp.einsum(
            "hdr,hg->hrgd", kv_basis[member], identity, preferred_element_type=jnp.float32
        )
        diagonal_block = diagonal_block.astype(jnp.bfloat16).reshape(
            head_count * rank_count, head_count * head_dim
        )
        empty_block = jnp.zeros_like(diagonal_block)
        if member == 0:
            blocks.append(jnp.concatenate([diagonal_block, empty_block], axis=0))
        else:
            blocks.append(jnp.concatenate([empty_block, diagonal_block], axis=0))
    return blocks


def rebuild(shared, packed, mapping):
    low_rank = jnp.dot(packed, mapping, preferred_element_type=jnp.float32)
    return (shared.astype(jnp.float32) + low_rank).astype(jnp.bfloat16)


def rebuild_pair(shared_keys, shared_values, packed, key_map, value_map):
    return (rebuild(shared_keys, packed, key_map), rebuild(shared_values, packed, value_map))


def attend(queries_here, shared_keys, shared_values, head_count):
    head_dim = queries_here.shape[1] // head_count
    score_scale = head_dim ** (-0.5)
    head_outputs = []
    for head_number in range(head_count):
        lower = head_number * head_dim
        queries_head = queries_here[:, lower : lower + head_dim]
        keys_head = shared_keys[:, lower : lower + head_dim]
        values_head = shared_values[:, lower : lower + head_dim]
        scores = (
            lax.dot_general(
                queries_head,
                keys_head,
                (((1,), (1,)), ((), ())),
                preferred_element_type=jnp.float32,
            )
            * score_scale
        )
        row_max = jnp.max(scores, axis=1, keepdims=True)
        exponent = jnp.exp(scores - row_max)
        row_total = jnp.sum(exponent, axis=1, keepdims=True)
        weights = exponent.astype(jnp.bfloat16)
        summed = jnp.dot(weights, values_head, preferred_element_type=jnp.float32)
        head_outputs.append((summed / row_total).astype(jnp.bfloat16))
    return jnp.concatenate(head_outputs, axis=1)


def per_device(
    queries, new_keys, new_values, prev_keys, prev_values, kv_basis, out_weight, out_gate
):
    step_count = queries.shape[0]
    local_rows = queries.shape[1]
    head_count = kv_basis.shape[1]
    offset = lax.axis_index("patch") * local_rows
    key_map, value_map = basis_maps(kv_basis)
    shared_keys, shared_values = (
        lax.all_gather(prev_keys, "patch", axis=0, tiled=True),
        lax.all_gather(prev_values, "patch", axis=0, tiled=True),
    )
    outputs = []
    for number in range(step_count):
        if number == 0:
            keys_here = prev_keys
            values_here = prev_values
        else:
            keys_here = take_rows(shared_keys, offset, local_rows)
            values_here = take_rows(shared_values, offset, local_rows)
        key_part = project(new_keys[number], keys_here, kv_basis[0], head_count)
        value_part = project(new_values[number], values_here, kv_basis[1], head_count)
        packed = jnp.stack([key_part, value_part], axis=1).reshape(local_rows, -1)
        everyone = lax.all_gather(packed, "patch", axis=0, tiled=True)
        shared_keys, shared_values = rebuild_pair(
            shared_keys, shared_values, everyone, key_map, value_map
        )
        attended = attend(queries[number], shared_keys, shared_values, head_count)
        partial_term = jnp.dot(attended, out_weight, preferred_element_type=jnp.float32)
        summed = lax.psum_scatter(
            partial_term.astype(jnp.bfloat16), "tp", scatter_dimension=1, tiled=True
        ).astype(jnp.float32)
        outputs.append((out_gate[number][None, :] * summed).astype(jnp.bfloat16))
    return jnp.stack(outputs)


def solution(mesh):
    placed = (
        P(None, "patch", "tp"),
        P(None, "patch", "tp"),
        P(None, "patch", "tp"),
        P("patch", "tp"),
        P("patch", "tp"),
        P(None, "tp", None, None),
        P("tp", None),
        P(None, "tp"),
    )
    return jax.shard_map(
        per_device, mesh=mesh, in_specs=placed, out_specs=P(None, "patch", "tp"), check_vma=False
    )
```

profile of v0, /device:TPU:1, one launch (start us, length us, event | category | flops | bytes accessed | tf_op | source)
XLA Modules:
  0.0 521.5 jit_solution(17558247553260546185)
XLA Ops:
  6.5 0.0 copy-start
  6.5 0.0 all-gather.3.cloned.1.call-start
  6.5 0.7 all-gather.3.cloned.1.call-update
  7.3 0.0 all-gather.5.cloned.1.call-start
  7.3 0.7 all-gather.5.cloned.1.call-update
  8.0 0.0 reduce-scatter.9.cloned.1.call-start
  8.1 0.9 fusion.4
  9.0 0.9 fusion.5
  9.9 0.1 reshape.42
  10.0 0.7 bitcast_convert_fusion.1
  10.7 0.1 multiply_convert_fusion.1
  10.9 0.7 slice_bitcast_fusion.1
  11.6 0.0 copy-start.4
  11.6 85.3 %all_gather.13 = bf16[2048,128]{1,0:T(8,128)(2,1)S(1)} all-gather(bf16[32,128]{1,0:T(8,128)(2,1)S(1)} %reshape.42), channel_id=1, replica_groups=mesh['patch'=64,'tp'=8] {'patch'}, dimensions={0}, use_global_device_ids=true | all-gather | bytes 532480 | tf_op jit(solution)/shard_map/all_gather | solution.py:100
  96.9 35.6 %all-gather.3.cloned.1.call-done = bf16[2048,256]{1,0:T(8,128)(2,1)} async-done(((bf16[32,256]{1,0:T(8,128)(2,1)}), bf16[2048,256]{1,0:T(8,128)(2,1)}) %all-gather.3.cloned.1.call-update) | async-done | bytes 1048592 | tf_op jit(solution)/shard_map/all_gather | solution.py:86
  132.5 1.6 fusion
  134.1 0.0 copy-done.4
  134.1 0.0 copy-done.5
  134.2 0.1 fusion.6
  134.3 1.6 fusion.80
  135.9 0.9 fusion.81
  136.9 112.4 %all-gather.5.cloned.1.call-done = bf16[2048,256]{1,0:T(8,128)(2,1)} async-done(((bf16[32,256]{1,0:T(8,128)(2,1)}), bf16[2048,256]{1,0:T(8,128)(2,1)}) %all-gather.5.cloned.1.call-update) | async-done | bytes 1048592 | tf_op jit(solution)/shard_map/all_gather | solution.py:87
  249.2 1.6 fusion.1
  250.9 0.0 copy-start.1
  250.9 1.0 copy-done.1
  251.9 0.0 copy-done.6
  251.9 0.1 fusion.7
  252.1 0.1 reshape.47
  252.2 78.8 %all_gather.15 = bf16[2048,128]{1,0:T(8,128)(2,1)S(1)} all-gather(bf16[32,128]{1,0:T(8,128)(2,1)S(1)} %reshape.47), channel_id=1, replica_groups=mesh['patch'=64,'tp'=8] {'patch'}, dimensions={0}, use_global_device_ids=true | all-gather | bytes 532480 | tf_op jit(solution)/shard_map/all_gather | solution.py:100
  331.0 1.6 fusion.3
  332.6 0.0 copy-start.3
  332.6 0.0 copy-start.9
  332.6 0.4 fusion.2
  333.0 0.0 copy-start.2
  333.0 0.4 fusion.78
  333.4 0.4 fusion.79
  333.8 0.0 copy-done.3
  333.8 0.0 copy-done.9
  333.8 0.2 fusion.22
  334.1 0.2 copy-done.2
  334.3 0.3 fusion.9
  334.6 0.2 fusion.26
  334.8 0.3 fusion.11
  335.1 0.2 fusion.24
  335.3 0.3 fusion.10
  335.6 0.0 copy-done
  335.6 0.0 copy-start.8
  335.6 0.4 convolution_convert_fusion
  336.0 1.2 copy.29
  337.1 0.0 reduce-scatter.9.cloned.1.call-update
  337.2 0.0 reduce-scatter.7.cloned.1.call-start
  337.2 0.0 copy-done.8
  337.2 0.2 fusion.20
  337.4 0.3 fusion.8
  337.7 0.0 copy-start.7
  337.7 0.4 convolution_convert_fusion.1
  338.1 1.2 copy.27
  339.3 0.0 reduce-scatter.7.cloned.1.call-update
  339.3 0.0 copy-done.7
  339.3 81.8 %reduce-scatter.9.cloned.1.call-done = bf16[384,32]{1,0:T(8,128)(2,1)} async-done(((bf16[3072,32]{1,0:T(8,128)(2,1)}), bf16[384,32]{1,0:T(8,128)(2,1)}) %reduce-scatter.9.cloned.1.call-update) | async-done | bytes 24592
  421.2 1.0 copy.30
  422.1 91.2 %reduce-scatter.7.cloned.1.call-done = bf16[384,32]{1,0:T(8,128)(2,1)} async-done(((bf16[3072,32]{1,0:T(8,128)(2,1)}), bf16[384,32]{1,0:T(8,128)(2,1)}) %reduce-scatter.7.cloned.1.call-update) | async-done | bytes 24592
  513.4 1.0 copy.28
  514.4 0.6 pad_maximum_fusion
  (12 shorter events, 0.1 us)
Async XLA Ops:
  6.5 329.0 %copy-start = (bf16[256,3072]{1,0:T(8,128)(2,1)S(1)}, bf16[256,3072]{1,0:T(8,128)(2,1)}, u32[]{:S(2)}) copy-start(bf16[256,3072]{1,0:T(8,128)(2,1)} %param.14) | copy-start | bytes 4718596
  6.5 126.0 %all-gather.3.cloned.1.call-start = ((), (), s32[]{:S(2)}) async-start(), calls=%async_computation.2 | async-start | bytes 1064960 | tf_op jit(solution)/shard_map/all_gather | solution.py:86
  7.3 242.0 %all-gather.5.cloned.1.call-start = ((), (), s32[]{:S(2)}) async-start(), calls=%async_computation.3 | async-start | bytes 1064960 | tf_op jit(solution)/shard_map/all_gather | solution.py:87
  8.0 413.2 %reduce-scatter.9.cloned.1.call-start = ((), (), s32[]{:S(2)}) async-start(), calls=%async_computation.5 | async-start | bytes 884736
  11.6 122.5 %copy-start.4 = (bf16[2,2,128,32]{2,3,1,0:T(8,128)(2,1)S(1)}, bf16[2,2,128,32]{2,3,1,0:T(8,128)(2,1)}, u32[]{:S(2)}) copy-start(bf16[2,2,128,32]{2,3,1,0:T(8,128)(2,1)} %param.13) | copy-start | bytes 98308
  11.6 122.5 %copy-start.5 = (bf16[2,32,256]{2,1,0:T(8,128)(2,1)S(1)}, bf16[2,32,256]{2,1,0:T(8,128)(2,1)}, u32[]{:S(2)}) copy-start(bf16[2,32,256]{2,1,0:T(8,128)(2,1)} %param.9) | copy-start | bytes 98308
  249.2 2.6 copy-start.6
  250.9 1.0 copy-start.1
  332.6 1.2 copy-start.3
  332.6 1.2 copy-start.9
  333.0 1.2 copy-start.2
  335.6 1.6 copy-start.8
  337.2 176.2 %reduce-scatter.7.cloned.1.call-start = ((), (), s32[]{:S(2)}) async-start(), calls=%async_computation.4 | async-start | bytes 884736
  337.7 1.6 copy-start.7
Sparse Core Ops, SparseCore 0:
  9.5 122.9 all-gather.2
  134.6 114.5 all-gather.4
  337.3 83.8 reduce-scatter.8
  425.5 87.8 reduce-scatter.6
where the time goes:
time: 523 us; the launch traced here: 522 us
  waiting for transfers between devices  322 us (62%)
  blocking collectives  164 us (31%)
  between operations  13.4 us (3%)
  matrix products  12.6 us (2%)
  local copies, waits for them, and re-layouts  6.53 us (1%)
    unnamed x6, waiting for transfers between devices  174 us
    all_gather x2, blocking collectives, per_device(): everyone = lax.all_gather(packed, 'patch', axis=0, tiled=True)  164 us
    all_gather x1, waiting for transfers between devices, per_device(): lax.all_gather(prev_values, 'patch', axis=0, tiled=True)  112 us
    all_gather x1, waiting for transfers between devices, per_device(): lax.all_gather(prev_keys, 'patch', axis=0, tiled=True)  35.6 us
  transfers between devices with their start and end apart: 4, of which 4 were waited for; matrix products, arithmetic and copies ran while one was open for 2% of the time, Pallas kernels for 0%

commit v1 on v0

v1 whole, which is shorter than its diff:
```python
import functools

import jax
import jax.numpy as jnp
from jax import lax
from jax.experimental import pallas as pl
from jax.experimental.pallas import tpu as pltpu
from jax.sharding import PartitionSpec as P

MESH = pl.DeviceIdType.MESH
NZ = 4
NY = 8
NX = 4
HD = 128
CHUNKS = 4
PER = NZ // CHUNKS
HALF = NY // 2


def slot_of(way, distance):
    if distance == 0 or distance == HALF:
        return 2 * distance - (distance == HALF)
    return 2 * distance - 1 + way


def far_way(chunk):
    return 0 if chunk < CHUNKS // 2 else 1


def nt_dot(a, b):
    return lax.dot_general(a, b, (((1,), (1,)), ((), ())), preferred_element_type=jnp.float32)


def nn_dot(a, b):
    return jnp.dot(a, b, preferred_element_type=jnp.float32)


def kernel(
    q_hbm, nk_hbm, nv_hbm, pk_hbm, pv_hbm, basis_hbm, w_hbm, out_ref,
    q_ref, nk_ref, nv_ref, pk_ref, pv_ref, basis_ref, w_ref,
    zsend, kv, qbuf, scores, weights, asend, abuf, hsend, hrecv,
    in_sem, zs_sem, zr_sem, qs_sem, qr_sem, rs_sem, rr_sem, cs_sem, cr_sem,
    fs_sem, fr_sem, as_sem, ar_sem, ws_sem, wr_sem, vs_sem, vr_sem, hs_sem, hr_sem,
):
    rows = pk_ref.shape[0]
    columns = out_ref.shape[2]
    patch, tp = lax.axis_index("patch"), lax.axis_index("tp")
    core = patch % 2
    y = (patch // 2) % NY
    z = patch // (2 * NY)
    x = tp % NX
    zh = tp // NX

    def at(z_to=None, y_to=None, core_to=None, x_to=None, zh_to=None):
        z_t = z if z_to is None else z_to
        y_t = y if y_to is None else y_to
        c_t = core if core_to is None else core_to
        x_t = x if x_to is None else x_to
        h_t = zh if zh_to is None else zh_to
        return ((z_t * NY + y_t) * 2 + c_t, h_t * NX + x_t)

    z_peers = [lax.rem(z + k, NZ) for k in range(NZ)]
    z_back = [lax.rem(z + NZ - k, NZ) for k in range(NZ)]
    x_peers = [lax.rem(x + k, NX) for k in range(NX)]
    x_back = [lax.rem(x + NX - k, NX) for k in range(NX)]
    y_next = [lax.rem(y + 1, NY), lax.rem(y + NY - 1, NY)]
    y_after = [lax.rem(y + 2, NY), lax.rem(y + NY - 2, NY)]

    halves = (1 - zh, zh)
    w_rows = w_hbm.shape[0]
    core_rows = pl.ds(pl.multiple_of(core * (w_rows // 2), w_rows // 2), w_rows // 2)

    def columns_of(which, x_to):
        return pl.ds(pl.multiple_of((halves[which] * NX + x_to) * columns, columns), columns)

    fetches = [
        pltpu.make_async_copy(source, target, in_sem.at[number])
        for number, (source, target) in enumerate(
            (
                (basis_hbm, basis_ref), (nk_hbm, nk_ref), (pk_hbm, pk_ref), (nv_hbm, nv_ref),
                (pv_hbm, pv_ref), (q_hbm, q_ref),
                (w_hbm.at[:, columns_of(0, x)], w_ref.at[0, x]), (w_hbm.at[:, columns_of(1, x)], w_ref.at[1, x]),
            )
        )
    ]
    for fetch in fetches:
        fetch.start()

    barrier = pltpu.get_barrier_semaphore()
    others = [(k, j) for k in range(NZ) for j in range(NX) if k or j]
    friends = [at(z_to=z_peers[k], x_to=x_peers[j]) for k, j in others]
    friends += [at(y_to=y_next[way]) for way in range(2)]
    friends += [at(y_to=y_after[way], core_to=c) for way in range(2) for c in (core, 1 - core)]
    friends += [at(core_to=1 - core), at(zh_to=1 - zh)]
    for friend in friends:
        pl.semaphore_signal(barrier, inc=1, device_id=friend, device_id_type=MESH)

    for fetch in fetches[:6]:
        fetch.wait()
    chains = [(member, head) for member in range(2) for head in range(2)]
    fresh_refs, prev_refs = (nk_ref, nv_ref), (pk_ref, pv_ref)
    columns_of_head = [slice(head * HD, (head + 1) * HD) for head in range(2)]
    basis = {(member, head): basis_ref[member, head] for member, head in chains}
    shared, mapped, shared_mapped = {}, {}, {}
    for member, head in chains:
        cols = columns_of_head[head]
        shared[member, head] = prev_refs[member][:, cols]
        fresh = fresh_refs[member]
        stacked = jnp.concatenate([fresh[0, :, cols], fresh[1, :, cols], shared[member, head]], axis=0)
        mapped[member, head] = nt_dot(stacked, basis[member, head])
        shared_mapped[member, head] = mapped[member, head][2 * rows :]
    for step in range(2):
        low_rank = {}
        for chain in chains:
            coefficients = mapped[chain][step * rows : (step + 1) * rows] - shared_mapped[chain]
            low_rank[chain] = nn_dot(coefficients.astype(jnp.bfloat16), basis[chain])
        for chain in chains:
            shared[chain] = (shared[chain].astype(jnp.float32) + low_rank[chain]).astype(jnp.bfloat16)
            if step == 0:
                shared_mapped[chain] = nt_dot(shared[chain], basis[chain])
        for member, head in chains:
            zsend[2 * head + step, member] = shared[member, head]
    for head in range(2):
        for step in range(2):
            zsend[2 * head + step, 2] = q_ref[step, :, head * HD : (head + 1) * HD]


    pl.semaphore_wait(barrier, len(friends))

    started = []

    def send(src, dst, send_sem, recv_sem, device):
        copy = pltpu.make_async_remote_copy(
            src_ref=src, dst_ref=dst, send_sem=send_sem, recv_sem=recv_sem, device_id=device, device_id_type=MESH
        )
        copy.start()
        started.append(copy)
        return copy

    z_copies, q_copies = {}, {}
    for k in range(1, NZ):
        z_copies[k] = send(
            zsend.at[z_peers[k], pl.ds(0, 2)], kv.at[0, 0, k], zs_sem.at[k], zr_sem.at[k], at(z_to=z_peers[k])
        )
    w_copies = {}
    for k in (2, 1, 3):
        for which in range(2):
            w_copies[k, which] = send(
                w_hbm.at[core_rows, columns_of(which, x_peers[k])], w_ref.at[which, x, core_rows],
                ws_sem.at[k, which], wr_sem.at[k, which], at(x_to=x_peers[k]),
            )
    kv[0, 0, 0] = zsend[z, 0:2]
    qbuf[0] = zsend[z, 2]

    ring, share, far_other = {}, {}, {}

    def push(way, distance, chunk, step):
        piece = pl.ds(chunk * PER, PER)
        ring[way, distance + step, chunk] = send(
            kv.at[0, slot_of(way, distance), piece],
            kv.at[0, slot_of(way, distance + step), piece],
            rs_sem.at[way, distance + step - 1, chunk],
            rr_sem.at[way, distance + step - 1, chunk],
            at(y_to=(y_next if step == 1 else y_after)[way]),
        )

    def far_push(way, chunk):
        push(way, HALF - 2, chunk, 2)
        piece = pl.ds(chunk * PER, PER)
        far_other[chunk] = send(
            kv.at[0, slot_of(way, HALF - 2), piece], kv.at[1, slot_of(0, HALF), piece],
            fs_sem.at[chunk], fr_sem.at[chunk], at(y_to=y_after[way], core_to=1 - core),
        )

    def share_core(way, distance, chunk):
        parts = 1 if distance < HALF - 1 else 2
        count = CHUNKS // parts
        if (chunk + 1) % count:
            return
        part = chunk // count
        piece = pl.ds(part * count * PER, count * PER)
        slot = slot_of(way, distance)
        share[slot, part] = send(
            kv.at[0, slot, piece],
            kv.at[1, slot, piece],
            cs_sem.at[slot, part],
            cr_sem.at[slot, part],
            at(core_to=1 - core),
        )

    lag = 2
    for chunk in range(CHUNKS + lag):
        if chunk < CHUNKS:
            for k in range(chunk * PER, (chunk + 1) * PER):
                if k:
                    z_copies[k].wait_recv()
            for way in range(2):
                push(way, 0, chunk, 2)
            share_core(0, 0, chunk)
        if chunk >= lag:
            for way in range(2):
                push(way, 0, chunk - lag, 1)
        if chunk == 0:
            for k in range(1, NZ):
                q_copies[k] = send(
                    zsend.at[z_peers[k], 2], qbuf.at[k], qs_sem.at[k], qr_sem.at[k], at(z_to=z_peers[k])
                )
    for k in range(1, NZ):
        q_copies[k].wait_recv()
    queries = qbuf[...].reshape(NZ * rows, HD)
    scale = HD ** (-0.5)
    block = NZ * rows
    lane_max = []

    def score(side, distance):
        first, last = slot_of(0, distance), slot_of(1, distance)
        count = last - first + 1
        keys = kv[side, first : last + 1, :, 0].reshape(count * block, HD)
        begin = (side * NY + first) * block
        found = nt_dot(queries, keys) * scale
        scores[:, begin : begin + count * block] = found
        for number in range(count):
            piece = found[:, number * block : (number + 1) * block]
            lane_max[:] = [jnp.maximum(lane_max[0], piece) if lane_max else piece]

    def score_other(distance):
        for slot in sorted({slot_of(0, distance), slot_of(1, distance)}):
            for part in range(2):
                if (slot, part) in share:
                    share[slot, part].wait_recv()
        for chunk in range(CHUNKS if distance == HALF else 0):
            far_other[chunk].wait_recv()
        score(1, distance)

    score(0, 0)
    for chunk in range(CHUNKS):
        for way in range(2):
            ring[way, HALF - 2, chunk].wait_recv()
            push(way, HALF - 2, chunk, 1)
        far_push(far_way(chunk), chunk)
        for way in range(2):
            share_core(way, HALF - 2, chunk)
    for chunk in range(CHUNKS):
        for way in range(2):
            ring[way, 1, chunk].wait_recv()
            share_core(way, 1, chunk)
    score(0, 2)
    score(0, 1)
    score_other(0)
    for chunk in range(CHUNKS):
        for way in range(2):
            ring[way, HALF - 1, chunk].wait_recv()
            share_core(way, HALF - 1, chunk)
    score_other(2)
    score_other(1)
    score(0, HALF - 1)
    for chunk in range(CHUNKS):
        ring[far_way(chunk), HALF, chunk].wait_recv()
    score(0, HALF)
    score_other(HALF)
    score_other(HALF - 1)

    row_max = jnp.max(lane_max[0], axis=1, keepdims=True)
    lane_total = jnp.zeros((block, block), jnp.float32)
    side_keys = NY * block
    summed = jnp.zeros((block, HD), jnp.float32)
    for side in range(2):
        for index in range(side * NY, (side + 1) * NY):
            span = slice(index * block, (index + 1) * block)
            exponent = jnp.exp(scores[:, span] - row_max)
            lane_total = lane_total + exponent
            weights[:, span] = exponent.astype(jnp.bfloat16)
        values = kv[side, :, :, 1].reshape(side_keys, HD)
        summed += nn_dot(weights[:, side * side_keys : (side + 1) * side_keys], values)
    row_total = jnp.sum(lane_total, axis=1, keepdims=True)
    attended = (summed / row_total).astype(jnp.bfloat16)
    asend[...] = attended.reshape(NZ, rows, HD)

    earlier = list(started)
    a_copies = {}
    for j in (2, 1, 3, 0):
        for k in (2, 1, 3, 0):
            if k or j:
                a_copies[k, j] = send(
                    asend.at[k], abuf.at[x, z], as_sem.at[k, j], ar_sem.at[k, j], at(z_to=z_back[k], x_to=x_peers[j])
                )
    abuf[x, z] = asend[0]

    v_copies = {}
    for which in range(2):
        for k in (1, 3, 2):
            w_copies[k, which].wait_recv()
            there = w_ref.at[which, x_back[k], core_rows]
            v_copies[k, which] = send(there, there, vs_sem.at[k, which], vr_sem.at[k, which], at(core_to=1 - core))
    for fetch in fetches[6:]:
        fetch.wait()
    for copy in earlier:
        copy.wait_send()
    for copy in a_copies.values():
        copy.wait_recv()
    by_step = [
        jnp.concatenate([abuf[j, 2 * head + step] for j in range(NX) for head in range(2)], axis=1) for step in range(2)
    ]
    features = jnp.concatenate(by_step, axis=0)

    def partial(which):
        for k in range(1, NX):
            v_copies[k, which].wait_recv()
        found = nn_dot(features, w_ref[which].reshape(NX * w_rows, columns))
        return found.reshape(2, rows, columns)

    there = partial(0)
    hsend[...] = there.astype(jnp.bfloat16)
    h_copies = []
    for step in range(2):
        h_copies.append(send(hsend.at[step], hrecv.at[step], hs_sem.at[step], hr_sem.at[step], at(zh_to=1 - zh)))
    here = partial(1)
    for copy in [*a_copies.values(), *v_copies.values()]:
        copy.wait_send()
    for step in range(2):
        h_copies[step].wait_recv()
        out_ref[step] = here[step] + hrecv[step].astype(jnp.float32)
    for copy in h_copies:
        copy.wait_send()


def per_device(queries, new_keys, new_values, prev_keys, prev_values, kv_basis, out_weight, out_gate):
    steps, rows, _ = queries.shape
    columns = out_gate.shape[1]
    bf16, f32 = jnp.bfloat16, jnp.float32
    vmem = pl.BlockSpec(memory_space=pltpu.VMEM)
    dma = pltpu.SemaphoreType.DMA
    tokens = 2 * NY * NZ * rows
    operands = (
        queries, new_keys, new_values, prev_keys, prev_values, jnp.swapaxes(kv_basis, 2, 3), out_weight,
    )
    summed = pl.pallas_call(
        kernel,
        out_shape=jax.ShapeDtypeStruct((steps, rows, columns), f32),
        in_specs=[pl.BlockSpec(memory_space=pltpu.HBM)] * 7,
        out_specs=vmem,
        scratch_shapes=[
            *[pltpu.VMEM(operand.shape, bf16) for operand in operands[:6]],
            pltpu.VMEM((2, NX, out_weight.shape[0], columns), bf16),
            pltpu.VMEM((NZ, 3, rows, HD), bf16),
            pltpu.VMEM((2, NY, NZ, 2, rows, HD), bf16),
            pltpu.VMEM((NZ, rows, HD), bf16),
            pltpu.VMEM((NZ * rows, tokens), f32),
            pltpu.VMEM((NZ * rows, tokens), bf16),
            pltpu.VMEM((NZ, rows, HD), bf16),
            pltpu.VMEM((NX, NZ, rows, HD), bf16),
            pltpu.VMEM((steps, rows, columns), bf16),
            pltpu.VMEM((steps, rows, columns), bf16),
            dma((8,)),
            dma((NZ,)), dma((NZ,)), dma((NZ,)), dma((NZ,)),
            dma((2, HALF, CHUNKS)), dma((2, HALF, CHUNKS)),
            dma((NY, 2)), dma((NY, 2)),
            dma((CHUNKS,)), dma((CHUNKS,)),
            dma((NZ, NX)), dma((NZ, NX)),
            dma((NX, 2)), dma((NX, 2)), dma((NX, 2)), dma((NX, 2)),
            dma((2,)), dma((2,)),
        ],
        compiler_params=pltpu.CompilerParams(
            collective_id=0, has_side_effects=True, vmem_limit_bytes=32 * 1024 * 1024
        ),
    )(*[pltpu.with_memory_space_constraint(operand, pltpu.HBM) for operand in operands])
    return (out_gate[:, None, :] * summed).astype(bf16)


def solution(mesh):
    placed = (
        P(None, "patch", "tp"),
        P(None, "patch", "tp"),
        P(None, "patch", "tp"),
        P("patch", "tp"),
        P("patch", "tp"),
        P(None, "tp", None, None),
        P("tp", None),
        P(None, "tp"),
    )
    return jax.shard_map(
        per_device, mesh=mesh, in_specs=placed, out_specs=P(None, "patch", "tp"), check_vma=False
    )
```

time: 523 us -> 41.6 us (0.08)
  waiting for transfers between devices: 322 us -> 0 us
  blocking collectives: 164 us -> 0 us
  Pallas kernels: 0 us -> 40.5 us
  between operations: 13.4 us -> 0.02 us
  matrix products: 12.6 us -> 0 us
  local copies, waits for them, and re-layouts: 6.53 us -> 0.01 us
    unnamed x6 -> x0, waiting for transfers between devices: 174 us -> none
    all_gather x2 -> x0, blocking collectives: 164 us -> none  [per_device(): everyone = lax.all_gather(packed, 'patch', axis=0, tiled=True)]
    all_gather x2 -> x0, waiting for transfers between devices: 148 us -> none  [the longest x1 112 us: per_device(): lax.all_gather(prev_values, 'patch', axis=0, tiled=True)]
    pallas_call x0 -> x1, Pallas kernels: none -> 40.5 us  [per_device(): pl.pallas_call(kernel, out_shape=jax.ShapeDtypeStruct((steps, rows, colum...]
    dot_general x18 -> x0, matrix products: 12.6 us -> none  [the longest x4 5.31 us: rebuild(): low_rank = jnp.dot(packed, mapping, preferred_element_type=jnp.float32)]
    unnamed x26 -> x2, local copies, waits for them, and re-layouts: 5.54 us -> 0.01 us
  transfers between devices with their start and end apart: 4 -> 0, of which waited for: 4 -> 0; matrix products, arithmetic and copies ran while one was open for 2% -> 0% of each run, Pallas kernels for 0% -> 0%
where the time goes in v1:
time: 41.6 us; the launch traced here: 41.2 us
  Pallas kernels  40.5 us (97%)
  other arithmetic  0.63 us (2%)
    pallas_call x1, Pallas kernels, per_device(): pl.pallas_call(kernel, out_shape=jax.ShapeDtypeStruct((steps, rows, colum...  40.5 us

profile of v1, /device:TPU:1, one launch (start us, length us, event | category | flops | bytes accessed | tf_op | source)
XLA Modules:
  0.0 41.2 jit_solution(10785552639827917746)
XLA Ops:
  0.0 0.0 copy-start
  0.0 40.5 %shard_map.82 = f32[2,32,384]{2,1,0:T(8,128)S(1)} custom-call(bf16[2,32,256]{2,1,0:T(8,128)(2,1)} %q_hbm.1, bf16[2,32,256]{2,1,0:T(8,128)(2,1)} %nk_hbm.1, bf16[2,32,256]{2,1,0:T(8,128)(2,1)} %nv_hbm.1, bf16[32,256]{1,0:T(8,128)(2,1)} %pk_hbm.1, bf16[32,256]{1,0:T(8,128)(2,1)} %pv_hbm.1, bf16[2,2,32,128]{3,2,1,0:T(8,128)(2,1)} %bitcast.1, ...), custom_call_target="tpu_custom_call" | custom-call | tf_op jit(solution)/shard_map/pallas_call | solution.py:337
  40.5 0.0 copy-done
  40.6 0.6 %multiply_convert_fusion = bf16[2,32,384]{2,1,0:T(8,128)(2,1)} fusion(f32[2,32,384]{2,1,0:T(8,128)S(1)} %shard_map.82, f32[2,384]{1,0:T(2,128)S(1)} %copy-done), kind=kLoop, calls=%fused_computation | loop fusion | flops 49152 | bytes 150528 | tf_op jit(solution)/shard_map/convert_element_type | solution.py:367
Async XLA Ops:
  0.0 40.5 %copy-start = (f32[2,384]{1,0:T(2,128)S(1)}, f32[2,384]{1,0:T(2,128)}, u32[]{:S(2)}) copy-start(f32[2,384]{1,0:T(2,128)} %param.15) | copy-start | bytes 9220

commit v2 on v1

--- a/solution.py
+++ b/solution.py
@@ -12,7 +12,7 @@
 NY = 8
 NX = 4
 HD = 128
-CHUNKS = 4
+CHUNKS = 2
 PER = NZ // CHUNKS
 HALF = NY // 2
 
@@ -89,8 +89,7 @@
     barrier = pltpu.get_barrier_semaphore()
     others = [(k, j) for k in range(NZ) for j in range(NX) if k or j]
     friends = [at(z_to=z_peers[k], x_to=x_peers[j]) for k, j in others]
-    friends += [at(y_to=y_next[way]) for way in range(2)]
-    friends += [at(y_to=y_after[way], core_to=c) for way in range(2) for c in (core, 1 - core)]
+    friends += [at(y_to=y_to[way], core_to=c) for y_to in (y_next, y_after) for way in range(2) for c in (core, 1 - core)]
     friends += [at(core_to=1 - core), at(zh_to=1 - zh)]
     for friend in friends:
         pl.semaphore_signal(barrier, inc=1, device_id=friend, device_id_type=MESH)
@@ -152,7 +151,7 @@
     kv[0, 0, 0] = zsend[z, 0:2]
     qbuf[0] = zsend[z, 2]
 
-    ring, share, far_other = {}, {}, {}
+    ring, share, cross = {}, {}, {}
 
     def push(way, distance, chunk, step):
         piece = pl.ds(chunk * PER, PER)
@@ -164,28 +163,19 @@
             at(y_to=(y_next if step == 1 else y_after)[way]),
         )
 
-    def far_push(way, chunk):
-        push(way, HALF - 2, chunk, 2)
+    def push_both(way, chunk, step):
+        push(way, HALF - 2, chunk, step)
         piece = pl.ds(chunk * PER, PER)
-        far_other[chunk] = send(
-            kv.at[0, slot_of(way, HALF - 2), piece], kv.at[1, slot_of(0, HALF), piece],
-            fs_sem.at[chunk], fr_sem.at[chunk], at(y_to=y_after[way], core_to=1 - core),
-        )
-
-    def share_core(way, distance, chunk):
-        parts = 1 if distance < HALF - 1 else 2
-        count = CHUNKS // parts
-        if (chunk + 1) % count:
-            return
-        part = chunk // count
-        piece = pl.ds(part * count * PER, count * PER)
-        slot = slot_of(way, distance)
-        share[slot, part] = send(
-            kv.at[0, slot, piece],
-            kv.at[1, slot, piece],
-            cs_sem.at[slot, part],
-            cr_sem.at[slot, part],
-            at(core_to=1 - core),
+        distance = HALF - 2 + step
+        cross[way, distance, chunk] = send(
+            kv.at[0, slot_of(way, HALF - 2), piece], kv.at[1, slot_of(way, distance), piece],
+            fs_sem.at[way, step - 1, chunk], fr_sem.at[way, step - 1, chunk],
+            at(y_to=(y_next if step == 1 else y_after)[way], core_to=1 - core),
+        )
+
+    def share_core(slot):
+        share[slot] = send(
+            kv.at[0, slot], kv.at[1, slot], cs_sem.at[slot], cr_sem.at[slot], at(core_to=1 - core)
         )
 
     lag = 2
@@ -196,7 +186,6 @@
                     z_copies[k].wait_recv()
             for way in range(2):
                 push(way, 0, chunk, 2)
-            share_core(0, 0, chunk)
         if chunk >= lag:
             for way in range(2):
                 push(way, 0, chunk - lag, 1)
@@ -205,6 +194,7 @@
                 q_copies[k] = send(
                     zsend.at[z_peers[k], 2], qbuf.at[k], qs_sem.at[k], qr_sem.at[k], at(z_to=z_peers[k])
                 )
+    share_core(0)
     for k in range(1, NZ):
         q_copies[k].wait_recv()
     queries = qbuf[...].reshape(NZ * rows, HD)
@@ -225,65 +215,62 @@
 
     def score_other(distance):
         for slot in sorted({slot_of(0, distance), slot_of(1, distance)}):
-            for part in range(2):
-                if (slot, part) in share:
-                    share[slot, part].wait_recv()
-        for chunk in range(CHUNKS if distance == HALF else 0):
-            far_other[chunk].wait_recv()
+            if slot in share:
+                share[slot].wait_recv()
+        for key, copy in cross.items():
+            if key[1] == distance:
+                copy.wait_recv()
         score(1, distance)
 
     score(0, 0)
     for chunk in range(CHUNKS):
         for way in range(2):
             ring[way, HALF - 2, chunk].wait_recv()
-            push(way, HALF - 2, chunk, 1)
-        far_push(far_way(chunk), chunk)
+            push_both(way, chunk, 1)
+        push_both(far_way(chunk), chunk, 2)
+    for distance in (2, 1):
         for way in range(2):
-            share_core(way, HALF - 2, chunk)
-    for chunk in range(CHUNKS):
-        for way in range(2):
-            ring[way, 1, chunk].wait_recv()
-            share_core(way, 1, chunk)
+            for chunk in range(CHUNKS if distance == 1 else 0):
+                ring[way, distance, chunk].wait_recv()
+            share_core(slot_of(way, distance))
     score(0, 2)
     score(0, 1)
-    score_other(0)
-    for chunk in range(CHUNKS):
-        for way in range(2):
-            ring[way, HALF - 1, chunk].wait_recv()
-            share_core(way, HALF - 1, chunk)
-    score_other(2)
-    score_other(1)
-    score(0, HALF - 1)
-    for chunk in range(CHUNKS):
-        ring[far_way(chunk), HALF, chunk].wait_recv()
-    score(0, HALF)
-    score_other(HALF)
-    score_other(HALF - 1)
-
-    row_max = jnp.max(lane_max[0], axis=1, keepdims=True)
-    lane_total = jnp.zeros((block, block), jnp.float32)
-    side_keys = NY * block
-    summed = jnp.zeros((block, HD), jnp.float32)
-    for side in range(2):
-        for index in range(side * NY, (side + 1) * NY):
-            span = slice(index * block, (index + 1) * block)
-            exponent = jnp.exp(scores[:, span] - row_max)
-            lane_total = lane_total + exponent
-            weights[:, span] = exponent.astype(jnp.bfloat16)
-        values = kv[side, :, :, 1].reshape(side_keys, HD)
-        summed += nn_dot(weights[:, side * side_keys : (side + 1) * side_keys], values)
-    row_total = jnp.sum(lane_total, axis=1, keepdims=True)
-    attended = (summed / row_total).astype(jnp.bfloat16)
-    asend[...] = attended.reshape(NZ, rows, HD)
+    for distance in range(HALF - 1):
+        score_other(distance)
+    for distance in (HALF - 1, HALF):
+        for key, copy in ring.items():
+            if key[1] == distance:
+                copy.wait_recv()
+        score(0, distance)
+        score_other(distance)
 
     earlier = list(started)
     a_copies = {}
-    for j in (2, 1, 3, 0):
-        for k in (2, 1, 3, 0):
-            if k or j:
-                a_copies[k, j] = send(
-                    asend.at[k], abuf.at[x, z], as_sem.at[k, j], ar_sem.at[k, j], at(z_to=z_back[k], x_to=x_peers[j])
-                )
+    side_keys = NY * block
+    part = block // 2
+    owners = NZ // 2
+    for half in (1, 0):
+        own_rows = slice(half * part, (half + 1) * part)
+        row_max = jnp.max(lane_max[0][own_rows], axis=1, keepdims=True)
+        lane_total = jnp.zeros((part, block), jnp.float32)
+        summed = jnp.zeros((part, HD), jnp.float32)
+        for side in range(2):
+            for index in range(side * NY, (side + 1) * NY):
+                span = slice(index * block, (index + 1) * block)
+                exponent = jnp.exp(scores[own_rows, span] - row_max)
+                lane_total = lane_total + exponent
+                weights[own_rows, span] = exponent.astype(jnp.bfloat16)
+            values = kv[side, :, :, 1].reshape(side_keys, HD)
+            summed += nn_dot(weights[own_rows, side * side_keys : (side + 1) * side_keys], values)
+        row_total = jnp.sum(lane_total, axis=1, keepdims=True)
+        attended = (summed / row_total).astype(jnp.bfloat16)
+        asend[half * owners : (half + 1) * owners] = attended.reshape(owners, rows, HD)
+        for j in (2, 1, 3, 0):
+            for k in range(half * owners, (half + 1) * owners):
+                if k or j:
+                    a_copies[k, j] = send(
+                        asend.at[k], abuf.at[x, z], as_sem.at[k, j], ar_sem.at[k, j], at(z_to=z_back[k], x_to=x_peers[j])
+                    )
     abuf[x, z] = asend[0]
 
     v_copies = {}
@@ -354,8 +341,8 @@
             dma((8,)),
             dma((NZ,)), dma((NZ,)), dma((NZ,)), dma((NZ,)),
             dma((2, HALF, CHUNKS)), dma((2, HALF, CHUNKS)),
-            dma((NY, 2)), dma((NY, 2)),
-            dma((CHUNKS,)), dma((CHUNKS,)),
+            dma((NY,)), dma((NY,)),
+            dma((2, 2, CHUNKS)), dma((2, 2, CHUNKS)),
             dma((NZ, NX)), dma((NZ, NX)),
             dma((NX, 2)), dma((NX, 2)), dma((NX, 2)), dma((NX, 2)),
             dma((2,)), dma((2,)),

time: 41.6 us -> 42.3 us (1.017)
  Pallas kernels: 40.5 us -> 41 us
    pallas_call x1, Pallas kernels: 40.5 us -> 41 us  [per_device(): pl.pallas_call(kernel, out_shape=jax.ShapeDtypeStruct((steps, rows, colum...]
where the time goes in v2:
time: 42.3 us; the launch traced here: 41.7 us
  Pallas kernels  41 us (97%)
  other arithmetic  0.63 us (1%)
    pallas_call x1, Pallas kernels, per_device(): pl.pallas_call(kernel, out_shape=jax.ShapeDtypeStruct((steps, rows, colum...  41 us

profile of v2, /device:TPU:1, one launch (start us, length us, event | category | flops | bytes accessed | tf_op | source)
XLA Modules:
  0.0 41.7 jit_solution(6387251538548574398)
XLA Ops:
  0.0 0.0 copy-start
  0.0 41.0 %shard_map.82 = f32[2,32,384]{2,1,0:T(8,128)S(1)} custom-call(bf16[2,32,256]{2,1,0:T(8,128)(2,1)} %q_hbm.1, bf16[2,32,256]{2,1,0:T(8,128)(2,1)} %nk_hbm.1, bf16[2,32,256]{2,1,0:T(8,128)(2,1)} %nv_hbm.1, bf16[32,256]{1,0:T(8,128)(2,1)} %pk_hbm.1, bf16[32,256]{1,0:T(8,128)(2,1)} %pv_hbm.1, bf16[2,2,32,128]{3,2,1,0:T(8,128)(2,1)} %bitcast.1, ...), custom_call_target="tpu_custom_call" | custom-call | tf_op jit(solution)/shard_map/pallas_call | solution.py:324
  41.0 0.0 copy-done
  41.0 0.6 %multiply_convert_fusion = bf16[2,32,384]{2,1,0:T(8,128)(2,1)} fusion(f32[2,32,384]{2,1,0:T(8,128)S(1)} %shard_map.82, f32[2,384]{1,0:T(2,128)S(1)} %copy-done), kind=kLoop, calls=%fused_computation | loop fusion | flops 49152 | bytes 150528 | tf_op jit(solution)/shard_map/convert_element_type | solution.py:354
Async XLA Ops:
  0.0 41.0 %copy-start = (f32[2,384]{1,0:T(2,128)S(1)}, f32[2,384]{1,0:T(2,128)}, u32[]{:S(2)}) copy-start(f32[2,384]{1,0:T(2,128)} %param.15) | copy-start | bytes 9220

commit v3 on v1

--- a/solution.py
+++ b/solution.py
@@ -12,7 +12,7 @@
 NY = 8
 NX = 4
 HD = 128
-CHUNKS = 4
+CHUNKS = 2
 PER = NZ // CHUNKS
 HALF = NY // 2
 
@@ -210,7 +210,10 @@
     queries = qbuf[...].reshape(NZ * rows, HD)
     scale = HD ** (-0.5)
     block = NZ * rows
-    lane_max = []
+    lane_max = {}
+
+    def group_of(distance):
+        return int(distance >= HALF - 1)
 
     def score(side, distance):
         first, last = slot_of(0, distance), slot_of(1, distance)
@@ -221,7 +224,8 @@
         scores[:, begin : begin + count * block] = found
         for number in range(count):
             piece = found[:, number * block : (number + 1) * block]
-            lane_max[:] = [jnp.maximum(lane_max[0], piece) if lane_max else piece]
+            group = group_of(distance)
+            lane_max[group] = jnp.maximum(lane_max[group], piece) if group in lane_max else piece
 
     def score_other(distance):
         for slot in sorted({slot_of(0, distance), slot_of(1, distance)}):
@@ -247,12 +251,34 @@
     score(0, 2)
     score(0, 1)
     score_other(0)
-    for chunk in range(CHUNKS):
-        for way in range(2):
-            ring[way, HALF - 1, chunk].wait_recv()
-            share_core(way, HALF - 1, chunk)
+    def weigh(group, row_max):
+        slots = [slot_of(way, distance) for distance in range(HALF + 1) for way in range(2) if group_of(distance) == group]
+        first, last = min(slots), max(slots)
+        count = last - first + 1
+        lane_total = jnp.zeros((block, block), jnp.float32)
+        summed = jnp.zeros((block, HD), jnp.float32)
+        for side in range(2):
+            begin = (side * NY + first) * block
+            for number in range(count):
+                span = slice(begin + number * block, begin + (number + 1) * block)
+                exponent = jnp.exp(scores[:, span] - row_max)
+                lane_total = lane_total + exponent
+                weights[:, span] = exponent.astype(jnp.bfloat16)
+            values = kv[side, first : last + 1, :, 1].reshape(count * block, HD)
+            summed = summed + nn_dot(weights[:, begin : begin + count * block], values)
+        return lane_total, summed
+
+    def share_last():
+        for chunk in range(CHUNKS):
+            for way in range(2):
+                ring[way, HALF - 1, chunk].wait_recv()
+                share_core(way, HALF - 1, chunk)
+
     score_other(2)
     score_other(1)
+    near_max = jnp.max(lane_max[0], axis=1, keepdims=True)
+    near_total, near_summed = weigh(0, near_max)
+    share_last()
     score(0, HALF - 1)
     for chunk in range(CHUNKS):
         ring[far_way(chunk), HALF, chunk].wait_recv()
@@ -260,20 +286,11 @@
     score_other(HALF)
     score_other(HALF - 1)
 
-    row_max = jnp.max(lane_max[0], axis=1, keepdims=True)
-    lane_total = jnp.zeros((block, block), jnp.float32)
-    side_keys = NY * block
-    summed = jnp.zeros((block, HD), jnp.float32)
-    for side in range(2):
-        for index in range(side * NY, (side + 1) * NY):
-            span = slice(index * block, (index + 1) * block)
-            exponent = jnp.exp(scores[:, span] - row_max)
-            lane_total = lane_total + exponent
-            weights[:, span] = exponent.astype(jnp.bfloat16)
-        values = kv[side, :, :, 1].reshape(side_keys, HD)
-        summed += nn_dot(weights[:, side * side_keys : (side + 1) * side_keys], values)
-    row_total = jnp.sum(lane_total, axis=1, keepdims=True)
-    attended = (summed / row_total).astype(jnp.bfloat16)
+    row_max = jnp.maximum(near_max, jnp.max(lane_max[1], axis=1, keepdims=True))
+    rescale = jnp.exp(near_max - row_max)
+    far_total, far_summed = weigh(1, row_max)
+    row_total = jnp.sum(near_total * rescale + far_total, axis=1, keepdims=True)
+    attended = ((near_summed * rescale + far_summed) / row_total).astype(jnp.bfloat16)
     asend[...] = attended.reshape(NZ, rows, HD)
 
     earlier = list(started)

time: 41.6 us -> 41.5 us (level)
  no operation moved by 1% of the time
where the time goes in v3:
time: 41.5 us; the launch traced here: 41.4 us
  Pallas kernels  40.7 us (98%)
  other arithmetic  0.63 us (2%)
    pallas_call x1, Pallas kernels, per_device(): pl.pallas_call(kernel, out_shape=jax.ShapeDtypeStruct((steps, rows, colum...  40.7 us

profile of v3, /device:TPU:1, one launch (start us, length us, event | category | flops | bytes accessed | tf_op | source)
XLA Modules:
  0.0 41.4 jit_solution(8793480161802706010)
XLA Ops:
  0.0 0.0 copy-start
  0.0 40.7 %shard_map.82 = f32[2,32,384]{2,1,0:T(8,128)S(1)} custom-call(bf16[2,32,256]{2,1,0:T(8,128)(2,1)} %q_hbm.1, bf16[2,32,256]{2,1,0:T(8,128)(2,1)} %nk_hbm.1, bf16[2,32,256]{2,1,0:T(8,128)(2,1)} %nv_hbm.1, bf16[32,256]{1,0:T(8,128)(2,1)} %pk_hbm.1, bf16[32,256]{1,0:T(8,128)(2,1)} %pv_hbm.1, bf16[2,2,32,128]{3,2,1,0:T(8,128)(2,1)} %bitcast.1, ...), custom_call_target="tpu_custom_call" | custom-call | tf_op jit(solution)/shard_map/pallas_call | solution.py:354
  40.8 0.0 copy-done
  40.8 0.6 %multiply_convert_fusion = bf16[2,32,384]{2,1,0:T(8,128)(2,1)} fusion(f32[2,32,384]{2,1,0:T(8,128)S(1)} %shard_map.82, f32[2,384]{1,0:T(2,128)S(1)} %copy-done), kind=kLoop, calls=%fused_computation | loop fusion | flops 49152 | bytes 150528 | tf_op jit(solution)/shard_map/convert_element_type | solution.py:384
Async XLA Ops:
  0.0 40.8 %copy-start = (f32[2,384]{1,0:T(2,128)S(1)}, f32[2,384]{1,0:T(2,128)}, u32[]{:S(2)}) copy-start(f32[2,384]{1,0:T(2,128)} %param.15) | copy-start | bytes 9220

commit v4 on v3

--- a/solution.py
+++ b/solution.py
@@ -143,8 +143,8 @@
             zsend.at[z_peers[k], pl.ds(0, 2)], kv.at[0, 0, k], zs_sem.at[k], zr_sem.at[k], at(z_to=z_peers[k])
         )
     w_copies = {}
-    for k in (2, 1, 3):
-        for which in range(2):
+    for which in range(2):
+        for k in (2, 1, 3):
             w_copies[k, which] = send(
                 w_hbm.at[core_rows, columns_of(which, x_peers[k])], w_ref.at[which, x, core_rows],
                 ws_sem.at[k, which], wr_sem.at[k, which], at(x_to=x_peers[k]),
@@ -293,7 +293,6 @@
     attended = ((near_summed * rescale + far_summed) / row_total).astype(jnp.bfloat16)
     asend[...] = attended.reshape(NZ, rows, HD)
 
-    earlier = list(started)
     a_copies = {}
     for j in (2, 1, 3, 0):
         for k in (2, 1, 3, 0):
@@ -304,41 +303,38 @@
     abuf[x, z] = asend[0]
 
     v_copies = {}
-    for which in range(2):
+
+    def share_weights(which):
         for k in (1, 3, 2):
             w_copies[k, which].wait_recv()
             there = w_ref.at[which, x_back[k], core_rows]
             v_copies[k, which] = send(there, there, vs_sem.at[k, which], vr_sem.at[k, which], at(core_to=1 - core))
-    for fetch in fetches[6:]:
-        fetch.wait()
-    for copy in earlier:
-        copy.wait_send()
+
+    def partial(which):
+        fetches[6 + which].wait()
+        for k in range(1, NX):
+            v_copies[k, which].wait_recv()
+        found = nn_dot(features, w_ref[which].reshape(NX * w_rows, columns))
+        return found.reshape(2, rows, columns)
+
+    share_weights(0)
     for copy in a_copies.values():
         copy.wait_recv()
     by_step = [
         jnp.concatenate([abuf[j, 2 * head + step] for j in range(NX) for head in range(2)], axis=1) for step in range(2)
     ]
     features = jnp.concatenate(by_step, axis=0)
-
-    def partial(which):
-        for k in range(1, NX):
-            v_copies[k, which].wait_recv()
-        found = nn_dot(features, w_ref[which].reshape(NX * w_rows, columns))
-        return found.reshape(2, rows, columns)
-
-    there = partial(0)
-    hsend[...] = there.astype(jnp.bfloat16)
+    hsend[...] = partial(0).astype(jnp.bfloat16)
     h_copies = []
     for step in range(2):
         h_copies.append(send(hsend.at[step], hrecv.at[step], hs_sem.at[step], hr_sem.at[step], at(zh_to=1 - zh)))
+    share_weights(1)
     here = partial(1)
-    for copy in [*a_copies.values(), *v_copies.values()]:
+    for copy in started:
         copy.wait_send()
     for step in range(2):
         h_copies[step].wait_recv()
         out_ref[step] = here[step] + hrecv[step].astype(jnp.float32)
-    for copy in h_copies:
-        copy.wait_send()
 
 
 def per_device(queries, new_keys, new_values, prev_keys, prev_values, kv_basis, out_weight, out_gate):

time: 41.5 us -> 41.8 us (level)
  no operation moved by 1% of the time
where the time goes in v4:
time: 41.8 us; the launch traced here: 41.4 us
  Pallas kernels  40.8 us (98%)
  other arithmetic  0.63 us (2%)
    pallas_call x1, Pallas kernels, per_device(): pl.pallas_call(kernel, out_shape=jax.ShapeDtypeStruct((steps, rows, colum...  40.8 us

profile of v4, /device:TPU:1, one launch (start us, length us, event | category | flops | bytes accessed | tf_op | source)
XLA Modules:
  0.0 41.4 jit_solution(569994351496495053)
XLA Ops:
  0.0 0.0 copy-start
  0.0 40.8 %shard_map.82 = f32[2,32,384]{2,1,0:T(8,128)S(1)} custom-call(bf16[2,32,256]{2,1,0:T(8,128)(2,1)} %q_hbm.1, bf16[2,32,256]{2,1,0:T(8,128)(2,1)} %nk_hbm.1, bf16[2,32,256]{2,1,0:T(8,128)(2,1)} %nv_hbm.1, bf16[32,256]{1,0:T(8,128)(2,1)} %pk_hbm.1, bf16[32,256]{1,0:T(8,128)(2,1)} %pv_hbm.1, bf16[2,2,32,128]{3,2,1,0:T(8,128)(2,1)} %bitcast.1, ...), custom_call_target="tpu_custom_call" | custom-call | tf_op jit(solution)/shard_map/pallas_call | solution.py:350
  40.8 0.0 copy-done
  40.8 0.6 %multiply_convert_fusion = bf16[2,32,384]{2,1,0:T(8,128)(2,1)} fusion(f32[2,32,384]{2,1,0:T(8,128)S(1)} %shard_map.82, f32[2,384]{1,0:T(2,128)S(1)} %copy-done), kind=kLoop, calls=%fused_computation | loop fusion | flops 49152 | bytes 150528 | tf_op jit(solution)/shard_map/convert_element_type | solution.py:380
Async XLA Ops:
  0.0 40.8 %copy-start = (f32[2,384]{1,0:T(2,128)S(1)}, f32[2,384]{1,0:T(2,128)}, u32[]{:S(2)}) copy-start(f32[2,384]{1,0:T(2,128)} %param.15) | copy-start | bytes 9220

commit v5 on v3

--- a/solution.py
+++ b/solution.py
@@ -38,7 +38,7 @@
 def kernel(
     q_hbm, nk_hbm, nv_hbm, pk_hbm, pv_hbm, basis_hbm, w_hbm, out_ref,
     q_ref, nk_ref, nv_ref, pk_ref, pv_ref, basis_ref, w_ref,
-    zsend, kv, qbuf, scores, weights, asend, abuf, hsend, hrecv,
+    diagonal, zsend, kv, qbuf, scores, weights, asend, abuf, hsend, hrecv,
     in_sem, zs_sem, zr_sem, qs_sem, qr_sem, rs_sem, rr_sem, cs_sem, cr_sem,
     fs_sem, fr_sem, as_sem, ar_sem, ws_sem, wr_sem, vs_sem, vr_sem, hs_sem, hr_sem,
 ):
@@ -87,39 +87,30 @@
         fetch.start()
 
     barrier = pltpu.get_barrier_semaphore()
-    others = [(k, j) for k in range(NZ) for j in range(NX) if k or j]
-    friends = [at(z_to=z_peers[k], x_to=x_peers[j]) for k, j in others]
-    friends += [at(y_to=y_next[way]) for way in range(2)]
-    friends += [at(y_to=y_after[way], core_to=c) for way in range(2) for c in (core, 1 - core)]
+    friends = [at(z_to=z_peers[k]) for k in range(1, NZ)] + [at(x_to=x_peers[k]) for k in range(1, NX)]
+    friends += [at(y_to=y_to[way]) for y_to in (y_next, y_after) for way in range(2)]
     friends += [at(core_to=1 - core), at(zh_to=1 - zh)]
     for friend in friends:
         pl.semaphore_signal(barrier, inc=1, device_id=friend, device_id_type=MESH)
 
+    diagonal[...] = jnp.zeros_like(diagonal)
     for fetch in fetches[:6]:
         fetch.wait()
-    chains = [(member, head) for member in range(2) for head in range(2)]
-    fresh_refs, prev_refs = (nk_ref, nv_ref), (pk_ref, pv_ref)
-    columns_of_head = [slice(head * HD, (head + 1) * HD) for head in range(2)]
-    basis = {(member, head): basis_ref[member, head] for member, head in chains}
-    shared, mapped, shared_mapped = {}, {}, {}
-    for member, head in chains:
-        cols = columns_of_head[head]
-        shared[member, head] = prev_refs[member][:, cols]
-        fresh = fresh_refs[member]
-        stacked = jnp.concatenate([fresh[0, :, cols], fresh[1, :, cols], shared[member, head]], axis=0)
-        mapped[member, head] = nt_dot(stacked, basis[member, head])
-        shared_mapped[member, head] = mapped[member, head][2 * rows :]
+    rank = basis_ref.shape[2]
+    for number in range(4):
+        diagonal[number * rank : (number + 1) * rank, number * HD : (number + 1) * HD] = basis_ref[number // 2, number % 2]
+    maps = diagonal[...]
+    shared = jnp.concatenate([pk_ref[...], pv_ref[...]], axis=1)
+    fresh = [jnp.concatenate([nk_ref[step], nv_ref[step]], axis=1) for step in range(2)]
+    mapped = nt_dot(jnp.concatenate([*fresh, shared], axis=0), maps)
+    shared_mapped = mapped[2 * rows :]
     for step in range(2):
-        low_rank = {}
-        for chain in chains:
-            coefficients = mapped[chain][step * rows : (step + 1) * rows] - shared_mapped[chain]
-            low_rank[chain] = nn_dot(coefficients.astype(jnp.bfloat16), basis[chain])
-        for chain in chains:
-            shared[chain] = (shared[chain].astype(jnp.float32) + low_rank[chain]).astype(jnp.bfloat16)
-            if step == 0:
-                shared_mapped[chain] = nt_dot(shared[chain], basis[chain])
-        for member, head in chains:
-            zsend[2 * head + step, member] = shared[member, head]
+        coefficients = (mapped[step * rows : (step + 1) * rows] - shared_mapped).astype(jnp.bfloat16)
+        shared = (shared.astype(jnp.float32) + nn_dot(coefficients, maps)).astype(jnp.bfloat16)
+        if step == 0:
+            shared_mapped = nt_dot(shared, maps)
+        for number in range(4):
+            zsend[2 * (number % 2) + step, number // 2] = shared[:, number * HD : (number + 1) * HD]
     for head in range(2):
         for step in range(2):
             zsend[2 * head + step, 2] = q_ref[step, :, head * HD : (head + 1) * HD]
@@ -359,6 +350,7 @@
         scratch_shapes=[
             *[pltpu.VMEM(operand.shape, bf16) for operand in operands[:6]],
             pltpu.VMEM((2, NX, out_weight.shape[0], columns), bf16),
+            pltpu.VMEM((4 * kv_basis.shape[3], 4 * HD), bf16),
             pltpu.VMEM((NZ, 3, rows, HD), bf16),
             pltpu.VMEM((2, NY, NZ, 2, rows, HD), bf16),
             pltpu.VMEM((NZ, rows, HD), bf16),

time: 41.5 us -> 40.6 us (0.978)
  Pallas kernels: 40.7 us -> 39.8 us
    pallas_call x1, Pallas kernels: 40.7 us -> 39.8 us  [per_device(): pl.pallas_call(kernel, out_shape=jax.ShapeDtypeStruct((steps, rows, colum...]
where the time goes in v5:
time: 40.6 us; the launch traced here: 40.5 us
  Pallas kernels  39.8 us (98%)
  other arithmetic  0.63 us (2%)
    pallas_call x1, Pallas kernels, per_device(): pl.pallas_call(kernel, out_shape=jax.ShapeDtypeStruct((steps, rows, colum...  39.8 us

profile of v5, /device:TPU:1, one launch (start us, length us, event | category | flops | bytes accessed | tf_op | source)
XLA Modules:
  0.0 40.5 jit_solution(11057066048025608668)
XLA Ops:
  0.0 0.0 copy-start
  0.0 39.8 %shard_map.82 = f32[2,32,384]{2,1,0:T(8,128)S(1)} custom-call(bf16[2,32,256]{2,1,0:T(8,128)(2,1)} %q_hbm.1, bf16[2,32,256]{2,1,0:T(8,128)(2,1)} %nk_hbm.1, bf16[2,32,256]{2,1,0:T(8,128)(2,1)} %nv_hbm.1, bf16[32,256]{1,0:T(8,128)(2,1)} %pk_hbm.1, bf16[32,256]{1,0:T(8,128)(2,1)} %pv_hbm.1, bf16[2,2,32,128]{3,2,1,0:T(8,128)(2,1)} %bitcast.1, ...), custom_call_target="tpu_custom_call" | custom-call | tf_op jit(solution)/shard_map/pallas_call | solution.py:345
  39.8 0.0 copy-done
  39.8 0.6 %multiply_convert_fusion = bf16[2,32,384]{2,1,0:T(8,128)(2,1)} fusion(f32[2,32,384]{2,1,0:T(8,128)S(1)} %shard_map.82, f32[2,384]{1,0:T(2,128)S(1)} %copy-done), kind=kLoop, calls=%fused_computation | loop fusion | flops 49152 | bytes 150528 | tf_op jit(solution)/shard_map/convert_element_type | solution.py:376
Async XLA Ops:
  0.0 39.8 %copy-start = (f32[2,384]{1,0:T(2,128)S(1)}, f32[2,384]{1,0:T(2,128)}, u32[]{:S(2)}) copy-start(f32[2,384]{1,0:T(2,128)} %param.15) | copy-start | bytes 9220

commit v6 on v5

--- a/solution.py
+++ b/solution.py
@@ -83,7 +83,7 @@
             )
         )
     ]
-    for fetch in fetches:
+    for fetch in fetches[:5]:
         fetch.start()
 
     barrier = pltpu.get_barrier_semaphore()
@@ -93,9 +93,23 @@
     for friend in friends:
         pl.semaphore_signal(barrier, inc=1, device_id=friend, device_id_type=MESH)
 
+    for fetch in fetches[5:]:
+        fetch.start()
     diagonal[...] = jnp.zeros_like(diagonal)
-    for fetch in fetches[:6]:
+    for fetch in fetches[:5]:
         fetch.wait()
+
+    def z_copy(pair, k):
+        return pltpu.make_async_remote_copy(
+            src_ref=zsend.at[pair, pl.ds(0, 2)], dst_ref=kv.at[0, 0, k],
+            send_sem=zs_sem.at[k], recv_sem=zr_sem.at[k], device_id=at(z_to=pair), device_id_type=MESH,
+        )
+
+    def send_pair(pair):
+        @pl.when(z != pair)
+        def _():
+            z_copy(pair, lax.rem(pair - z + NZ, NZ)).start()
+
     rank = basis_ref.shape[2]
     for number in range(4):
         diagonal[number * rank : (number + 1) * rank, number * HD : (number + 1) * HD] = basis_ref[number // 2, number % 2]
@@ -111,28 +125,30 @@
             shared_mapped = nt_dot(shared, maps)
         for number in range(4):
             zsend[2 * (number % 2) + step, number // 2] = shared[:, number * HD : (number + 1) * HD]
+        if step == 0:
+            pl.semaphore_wait(barrier, len(friends))
+        for head in range(2):
+            send_pair(2 * head + step)
+
+    started = []
+
+    def send(src, dst, send_sem, recv_sem, device):
+        copy = pltpu.make_async_remote_copy(
+            src_ref=src, dst_ref=dst, send_sem=send_sem, recv_sem=recv_sem, device_id=device, device_id_type=MESH
+        )
+        copy.start()
+        started.append(copy)
+        return copy
+
+    z_copies, q_copies = {}, {}
+    for k in range(1, NZ):
+        z_copies[k] = z_copy(z_peers[k], k)
+        started.append(z_copies[k])
+    kv[0, 0, 0] = zsend[z, 0:2]
+    fetches[5].wait()
     for head in range(2):
         for step in range(2):
             zsend[2 * head + step, 2] = q_ref[step, :, head * HD : (head + 1) * HD]
-
-
-    pl.semaphore_wait(barrier, len(friends))
-
-    started = []
-
-    def send(src, dst, send_sem, recv_sem, device):
-        copy = pltpu.make_async_remote_copy(
-            src_ref=src, dst_ref=dst, send_sem=send_sem, recv_sem=recv_sem, device_id=device, device_id_type=MESH
-        )
-        copy.start()
-        started.append(copy)
-        return copy
-
-    z_copies, q_copies = {}, {}
-    for k in range(1, NZ):
-        z_copies[k] = send(
-            zsend.at[z_peers[k], pl.ds(0, 2)], kv.at[0, 0, k], zs_sem.at[k], zr_sem.at[k], at(z_to=z_peers[k])
-        )
     w_copies = {}
     for k in (2, 1, 3):
         for which in range(2):
@@ -140,7 +156,6 @@
                 w_hbm.at[core_rows, columns_of(which, x_peers[k])], w_ref.at[which, x, core_rows],
                 ws_sem.at[k, which], wr_sem.at[k, which], at(x_to=x_peers[k]),
             )
-    kv[0, 0, 0] = zsend[z, 0:2]
     qbuf[0] = zsend[z, 2]
 
     ring, share, far_other = {}, {}, {}

time: 40.6 us -> 40.3 us (level)
  no operation moved by 1% of the time
where the time goes in v6:
time: 40.3 us; the launch traced here: 40.2 us
  Pallas kernels  39.5 us (98%)
  other arithmetic  0.63 us (2%)
    pallas_call x1, Pallas kernels, per_device(): pl.pallas_call(kernel, out_shape=jax.ShapeDtypeStruct((steps, rows, colum...  39.5 us

profile of v6, /device:TPU:1, one launch (start us, length us, event | category | flops | bytes accessed | tf_op | source)
XLA Modules:
  0.0 40.2 jit_solution(8661760897418023349)
XLA Ops:
  0.0 0.0 copy-start
  0.0 39.5 %shard_map.82 = f32[2,32,384]{2,1,0:T(8,128)S(1)} custom-call(bf16[2,32,256]{2,1,0:T(8,128)(2,1)} %q_hbm.1, bf16[2,32,256]{2,1,0:T(8,128)(2,1)} %nk_hbm.1, bf16[2,32,256]{2,1,0:T(8,128)(2,1)} %nv_hbm.1, bf16[32,256]{1,0:T(8,128)(2,1)} %pk_hbm.1, bf16[32,256]{1,0:T(8,128)(2,1)} %pv_hbm.1, bf16[2,2,32,128]{3,2,1,0:T(8,128)(2,1)} %bitcast.1, ...), custom_call_target="tpu_custom_call" | custom-call | tf_op jit(solution)/shard_map/pallas_call | solution.py:360
  39.6 0.0 copy-done
  39.6 0.6 %multiply_convert_fusion = bf16[2,32,384]{2,1,0:T(8,128)(2,1)} fusion(f32[2,32,384]{2,1,0:T(8,128)S(1)} %shard_map.82, f32[2,384]{1,0:T(2,128)S(1)} %copy-done), kind=kLoop, calls=%fused_computation | loop fusion | flops 49152 | bytes 150528 | tf_op jit(solution)/shard_map/convert_element_type | solution.py:391
Async XLA Ops:
  0.0 39.6 %copy-start = (f32[2,384]{1,0:T(2,128)S(1)}, f32[2,384]{1,0:T(2,128)}, u32[]{:S(2)}) copy-start(f32[2,384]{1,0:T(2,128)} %param.15) | copy-start | bytes 9220

commit v7 on v6

--- a/solution.py
+++ b/solution.py
@@ -257,21 +257,21 @@
     score(0, 2)
     score(0, 1)
     score_other(0)
-    def weigh(group, row_max):
+    def weigh(group, row_max, own_rows):
         slots = [slot_of(way, distance) for distance in range(HALF + 1) for way in range(2) if group_of(distance) == group]
         first, last = min(slots), max(slots)
         count = last - first + 1
-        lane_total = jnp.zeros((block, block), jnp.float32)
-        summed = jnp.zeros((block, HD), jnp.float32)
+        lane_total = jnp.zeros((row_max.shape[0], block), jnp.float32)
+        summed = jnp.zeros((row_max.shape[0], HD), jnp.float32)
         for side in range(2):
             begin = (side * NY + first) * block
             for number in range(count):
                 span = slice(begin + number * block, begin + (number + 1) * block)
-                exponent = jnp.exp(scores[:, span] - row_max)
+                exponent = jnp.exp(scores[own_rows, span] - row_max)
                 lane_total = lane_total + exponent
-                weights[:, span] = exponent.astype(jnp.bfloat16)
+                weights[own_rows, span] = exponent.astype(jnp.bfloat16)
             values = kv[side, first : last + 1, :, 1].reshape(count * block, HD)
-            summed = summed + nn_dot(weights[:, begin : begin + count * block], values)
+            summed = summed + nn_dot(weights[own_rows, begin : begin + count * block], values)
         return lane_total, summed
 
     def share_last():
@@ -283,7 +283,7 @@
     score_other(2)
     score_other(1)
     near_max = jnp.max(lane_max[0], axis=1, keepdims=True)
-    near_total, near_summed = weigh(0, near_max)
+    near_total, near_summed = weigh(0, near_max, slice(0, block))
     share_last()
     score(0, HALF - 1)
     for chunk in range(CHUNKS):
@@ -292,21 +292,23 @@
     score_other(HALF)
     score_other(HALF - 1)
 
-    row_max = jnp.maximum(near_max, jnp.max(lane_max[1], axis=1, keepdims=True))
-    rescale = jnp.exp(near_max - row_max)
-    far_total, far_summed = weigh(1, row_max)
-    row_total = jnp.sum(near_total * rescale + far_total, axis=1, keepdims=True)
-    attended = ((near_summed * rescale + far_summed) / row_total).astype(jnp.bfloat16)
-    asend[...] = attended.reshape(NZ, rows, HD)
-
     earlier = list(started)
     a_copies = {}
-    for j in (2, 1, 3, 0):
-        for k in (2, 1, 3, 0):
-            if k or j:
-                a_copies[k, j] = send(
-                    asend.at[k], abuf.at[x, z], as_sem.at[k, j], ar_sem.at[k, j], at(z_to=z_back[k], x_to=x_peers[j])
-                )
+    part, owners = block // 2, NZ // 2
+    all_max = jnp.maximum(near_max, jnp.max(lane_max[1], axis=1, keepdims=True))
+    for half in (1, 0):
+        own_rows = slice(half * part, (half + 1) * part)
+        rescale = jnp.exp(near_max[own_rows] - all_max[own_rows])
+        far_total, far_summed = weigh(1, all_max[own_rows], own_rows)
+        row_total = jnp.sum(near_total[own_rows] * rescale + far_total, axis=1, keepdims=True)
+        attended = ((near_summed[own_rows] * rescale + far_summed) / row_total).astype(jnp.bfloat16)
+        asend[half * owners : (half + 1) * owners] = attended.reshape(owners, rows, HD)
+        for j in (2, 1, 3, 0):
+            for k in range(half * owners, (half + 1) * owners):
+                if k or j:
+                    a_copies[k, j] = send(
+                        asend.at[k], abuf.at[x, z], as_sem.at[k, j], ar_sem.at[k, j], at(z_to=z_back[k], x_to=x_peers[j])
+                    )
     abuf[x, z] = asend[0]
 
     v_copies = {}

time: 40.3 us -> 40 us (level)
  no operation moved by 1% of the time
where the time goes in v7:
time: 40 us; the launch traced here: 39.9 us
  Pallas kernels  39.2 us (98%)
  other arithmetic  0.63 us (2%)
    pallas_call x1, Pallas kernels, per_device(): pl.pallas_call(kernel, out_shape=jax.ShapeDtypeStruct((steps, rows, colum...  39.2 us

profile of v7, /device:TPU:1, one launch (start us, length us, event | category | flops | bytes accessed | tf_op | source)
XLA Modules:
  0.0 39.9 jit_solution(16846872483020462208)
XLA Ops:
  0.0 0.0 copy-start
  0.0 39.2 %shard_map.82 = f32[2,32,384]{2,1,0:T(8,128)S(1)} custom-call(bf16[2,32,256]{2,1,0:T(8,128)(2,1)} %q_hbm.1, bf16[2,32,256]{2,1,0:T(8,128)(2,1)} %nk_hbm.1, bf16[2,32,256]{2,1,0:T(8,128)(2,1)} %nv_hbm.1, bf16[32,256]{1,0:T(8,128)(2,1)} %pk_hbm.1, bf16[32,256]{1,0:T(8,128)(2,1)} %pv_hbm.1, bf16[2,2,32,128]{3,2,1,0:T(8,128)(2,1)} %bitcast.1, ...), custom_call_target="tpu_custom_call" | custom-call | tf_op jit(solution)/shard_map/pallas_call | solution.py:362
  39.2 0.0 copy-done
  39.3 0.6 %multiply_convert_fusion = bf16[2,32,384]{2,1,0:T(8,128)(2,1)} fusion(f32[2,32,384]{2,1,0:T(8,128)S(1)} %shard_map.82, f32[2,384]{1,0:T(2,128)S(1)} %copy-done), kind=kLoop, calls=%fused_computation | loop fusion | flops 49152 | bytes 150528 | tf_op jit(solution)/shard_map/convert_element_type | solution.py:393
Async XLA Ops:
  0.0 39.2 %copy-start = (f32[2,384]{1,0:T(2,128)S(1)}, f32[2,384]{1,0:T(2,128)}, u32[]{:S(2)}) copy-start(f32[2,384]{1,0:T(2,128)} %param.15) | copy-start | bytes 9220

commit v8 on v7

--- a/solution.py
+++ b/solution.py
@@ -149,6 +149,8 @@
     for head in range(2):
         for step in range(2):
             zsend[2 * head + step, 2] = q_ref[step, :, head * HD : (head + 1) * HD]
+    for k in range(1, NZ):
+        q_copies[k] = send(zsend.at[z_peers[k], 2], qbuf.at[k], qs_sem.at[k], qr_sem.at[k], at(z_to=z_peers[k]))
     w_copies = {}
     for k in (2, 1, 3):
         for which in range(2):
@@ -206,14 +208,6 @@
         if chunk >= lag:
             for way in range(2):
                 push(way, 0, chunk - lag, 1)
-        if chunk == 0:
-            for k in range(1, NZ):
-                q_copies[k] = send(
-                    zsend.at[z_peers[k], 2], qbuf.at[k], qs_sem.at[k], qr_sem.at[k], at(z_to=z_peers[k])
-                )
-    for k in range(1, NZ):
-        q_copies[k].wait_recv()
-    queries = qbuf[...].reshape(NZ * rows, HD)
     scale = HD ** (-0.5)
     block = NZ * rows
     lane_max = {}
@@ -242,7 +236,6 @@
             far_other[chunk].wait_recv()
         score(1, distance)
 
-    score(0, 0)
     for chunk in range(CHUNKS):
         for way in range(2):
             ring[way, HALF - 2, chunk].wait_recv()
@@ -250,6 +243,10 @@
         far_push(far_way(chunk), chunk)
         for way in range(2):
             share_core(way, HALF - 2, chunk)
+    for k in range(1, NZ):
+        q_copies[k].wait_recv()
+    queries = qbuf[...].reshape(NZ * rows, HD)
+    score(0, 0)
     for chunk in range(CHUNKS):
         for way in range(2):
             ring[way, 1, chunk].wait_recv()

time: 40 us -> 40.4 us (1.010)
  no operation moved by 1% of the time
where the time goes in v8:
time: 40.4 us; the launch traced here: 40.3 us
  Pallas kernels  39.6 us (98%)
  other arithmetic  0.63 us (2%)
    pallas_call x1, Pallas kernels, per_device(): pl.pallas_call(kernel, out_shape=jax.ShapeDtypeStruct((steps, rows, colum...  39.6 us

profile of v8, /device:TPU:1, one launch (start us, length us, event | category | flops | bytes accessed | tf_op | source)
XLA Modules:
  0.0 40.3 jit_solution(17077728391303414953)
XLA Ops:
  0.0 0.0 copy-start
  0.0 39.6 %shard_map.82 = f32[2,32,384]{2,1,0:T(8,128)S(1)} custom-call(bf16[2,32,256]{2,1,0:T(8,128)(2,1)} %q_hbm.1, bf16[2,32,256]{2,1,0:T(8,128)(2,1)} %nk_hbm.1, bf16[2,32,256]{2,1,0:T(8,128)(2,1)} %nv_hbm.1, bf16[32,256]{1,0:T(8,128)(2,1)} %pk_hbm.1, bf16[32,256]{1,0:T(8,128)(2,1)} %pv_hbm.1, bf16[2,2,32,128]{3,2,1,0:T(8,128)(2,1)} %bitcast.1, ...), custom_call_target="tpu_custom_call" | custom-call | tf_op jit(solution)/shard_map/pallas_call | solution.py:359
  39.6 0.0 copy-done
  39.6 0.6 %multiply_convert_fusion = bf16[2,32,384]{2,1,0:T(8,128)(2,1)} fusion(f32[2,32,384]{2,1,0:T(8,128)S(1)} %shard_map.82, f32[2,384]{1,0:T(2,128)S(1)} %copy-done), kind=kLoop, calls=%fused_computation | loop fusion | flops 49152 | bytes 150528 | tf_op jit(solution)/shard_map/convert_element_type | solution.py:390
Async XLA Ops:
  0.0 39.6 %copy-start = (f32[2,384]{1,0:T(2,128)S(1)}, f32[2,384]{1,0:T(2,128)}, u32[]{:S(2)}) copy-start(f32[2,384]{1,0:T(2,128)} %param.15) | copy-start | bytes 9220

commit v9 on v7

--- a/solution.py
+++ b/solution.py
@@ -319,8 +319,6 @@
             v_copies[k, which] = send(there, there, vs_sem.at[k, which], vr_sem.at[k, which], at(core_to=1 - core))
     for fetch in fetches[6:]:
         fetch.wait()
-    for copy in earlier:
-        copy.wait_send()
     for copy in a_copies.values():
         copy.wait_recv()
     by_step = [
@@ -340,6 +338,8 @@
     for step in range(2):
         h_copies.append(send(hsend.at[step], hrecv.at[step], hs_sem.at[step], hr_sem.at[step], at(zh_to=1 - zh)))
     here = partial(1)
+    for copy in earlier:
+        copy.wait_send()
     for copy in [*a_copies.values(), *v_copies.values()]:
         copy.wait_send()
     for step in range(2):

time: 40 us -> 40 us (level)
  no operation moved by 1% of the time
where the time goes in v9:
time: 40 us; the launch traced here: 39.9 us
  Pallas kernels  39.2 us (98%)
  other arithmetic  0.63 us (2%)
    pallas_call x1, Pallas kernels, per_device(): pl.pallas_call(kernel, out_shape=jax.ShapeDtypeStruct((steps, rows, colum...  39.2 us

profile of v9, /device:TPU:1, one launch (start us, length us, event | category | flops | bytes accessed | tf_op | source)
XLA Modules:
  0.0 39.9 jit_solution(2814125214529408704)
XLA Ops:
  0.0 0.0 copy-start
  0.0 39.2 %shard_map.82 = f32[2,32,384]{2,1,0:T(8,128)S(1)} custom-call(bf16[2,32,256]{2,1,0:T(8,128)(2,1)} %q_hbm.1, bf16[2,32,256]{2,1,0:T(8,128)(2,1)} %nk_hbm.1, bf16[2,32,256]{2,1,0:T(8,128)(2,1)} %nv_hbm.1, bf16[32,256]{1,0:T(8,128)(2,1)} %pk_hbm.1, bf16[32,256]{1,0:T(8,128)(2,1)} %pv_hbm.1, bf16[2,2,32,128]{3,2,1,0:T(8,128)(2,1)} %bitcast.1, ...), custom_call_target="tpu_custom_call" | custom-call | tf_op jit(solution)/shard_map/pallas_call | solution.py:362
  39.2 0.0 copy-done
  39.3 0.6 %multiply_convert_fusion = bf16[2,32,384]{2,1,0:T(8,128)(2,1)} fusion(f32[2,32,384]{2,1,0:T(8,128)S(1)} %shard_map.82, f32[2,384]{1,0:T(2,128)S(1)} %copy-done), kind=kLoop, calls=%fused_computation | loop fusion | flops 49152 | bytes 150528 | tf_op jit(solution)/shard_map/convert_element_type | solution.py:393
Async XLA Ops:
  0.0 39.2 %copy-start = (f32[2,384]{1,0:T(2,128)S(1)}, f32[2,384]{1,0:T(2,128)}, u32[]{:S(2)}) copy-start(f32[2,384]{1,0:T(2,128)} %param.15) | copy-start | bytes 9220
